TPU v7x, 32 devices: a whole 2x2x4 slice. The times are simulated.
32 devices in a mesh: group: 2 (over y), row: 4 (over z), cent: 4 (over x, core).
Axes of the slice: x: 2, y: 2, z: 4, core: 2. Of those that a mesh axis runs over, the one named last changes fastest.
Arguments:
- embeddings: bfloat16 [8, 512, 1024], P(('group', 'cent'), 'row'), parts along dimension 0, may hold values from -6 to 6
- centroids: bfloat16 [8, 2048, 1024], P(('group', 'cent'), 'row'), parts along dimension 0, may hold values from -1 to 1
- owner: int32 [8, 512, 1], P(('group', 'cent'), 'row'), parts along dimension 0, may hold values from 0 to 3; in each aligned block of 128 rows (0 to 127, 128 to 255, ..., all dimensions but the last counted through in order) at most 128 rows name the same one
- slot: int32 [8, 512], P(('group', 'cent'), 'row'), parts along dimension 0, may hold values from 0 to 511
Outputs:
- gap: float32 [8, 512], P(('group', 'cent'), 'row'), parts along dimension 0
- new_centroids: float32 [8, 2048, 1024], P(('group', 'cent'), 'row'), parts along dimension 0
There are 2 independent parts, one for each index of `group`. A program takes and returns all parts, laid end to end along the dimension named above; each array names one. Nothing has to cross between parts.
Inputs may be any that keep to these rules, and one draw needn't show every extreme that they name: Among the 128 rows of one device, at most 128 have the same owner, and in every draw some device has exactly 128 rows with one owner.
All inputs are finite; a program needn't handle non-finite values.
Results may differ from a plain program's by a relative error of at most 0.0003.
Values may be sent and summed in bfloat16 or wider, within the bound.
A program may use at most 64 MiB of HBM per device.

v0:
```python
import jax
import jax.numpy as jnp
from jax import lax
from jax.sharding import PartitionSpec as P


def combined_all(part, axis, combine):
    gathered = jax.tree.map(lambda a: lax.all_gather(a, axis), part)

    def take(source):
        return jax.tree.map(lambda a: lax.dynamic_index_in_dim(a, source, 0, False), gathered)

    return lax.fori_loop(
        1, lax.axis_size(axis), lambda source, state: combine(state, take(source)), take(0)
    )


def score_piece(piece_rows, piece_owner, piece_slot, cent_block, half_norm, my_index):
    scores = lax.dot_general(
        piece_rows, cent_block, (((1,), (1,)), ((), ())), preferred_element_type=jnp.float32
    )
    scores = scores - half_norm[None, :]
    best_part = jnp.max(scores, axis=1)
    column_ids = lax.broadcasted_iota(jnp.int32, scores.shape, 1)
    picked = (piece_slot[:, None] == column_ids) & (piece_owner[:, None] == my_index)
    chosen_part = jnp.sum(jnp.where(picked, scores, jnp.zeros_like(scores)), axis=1)
    return (best_part, chosen_part)


def member_sums(piece_rows, piece_owner, piece_slot, cent_count, my_index):
    member = (
        lax.broadcasted_iota(jnp.int32, (cent_count, piece_rows.shape[0]), 0) == piece_slot[None, :]
    ) & (piece_owner[None, :] == my_index)
    sums = jnp.dot(member.astype(jnp.bfloat16), piece_rows, preferred_element_type=jnp.float32)
    counts = jnp.sum(member.astype(jnp.float32), axis=1)
    return (sums, counts)


def combine_best(first_pair, second_pair):
    return (jnp.maximum(first_pair[0], second_pair[0]), first_pair[1] + second_pair[1])


def body(embeddings, centroids, owner, slot):
    embed_rows = embeddings[0]
    cent_block = centroids[0]
    owner_ids = owner[0, :, 0]
    slot_ids = slot[0]
    my_index = lax.axis_index("row")
    count_dev = embed_rows.shape[0]
    cent_count = cent_block.shape[0]
    half_norm = 0.5 * jnp.sum(jnp.square(cent_block.astype(jnp.float32)), axis=1)
    all_embed, all_owner, all_slot = (
        lax.all_gather(embed_rows, "row", axis=0, tiled=True),
        lax.all_gather(owner_ids, "row", axis=0, tiled=True),
        lax.all_gather(slot_ids, "row", axis=0, tiled=True),
    )
    best_local, chosen_local = score_piece(
        all_embed, all_owner, all_slot, cent_block, half_norm, my_index
    )
    sums, counts = member_sums(all_embed, all_owner, all_slot, cent_count, my_index)
    updated = (cent_block.astype(jnp.float32) + sums) / (1.0 + counts)[:, None]
    best_all, chosen_all = combined_all((best_local, chosen_local), "row", combine_best)
    best_mine = lax.dynamic_slice_in_dim(best_all, my_index * count_dev, count_dev, 0)
    chosen_mine = lax.dynamic_slice_in_dim(chosen_all, my_index * count_dev, count_dev, 0)
    gap_rows = (best_mine - chosen_mine)[None, :]
    return (gap_rows, updated[None, :, :])


def solution(mesh):
    placed = (
        P(("group", "cent"), "row", None),
        P(("group", "cent"), "row", None),
        P(("group", "cent"), "row", None),
        P(("group", "cent"), "row"),
    )
    return jax.shard_map(
        body,
        mesh=mesh,
        in_specs=placed,
        out_specs=(P(("group", "cent"), "row"), P(("group", "cent"), "row", None)),
        check_vma=False,
    )
```

profile of v0, /device:TPU:0, one launch (start us, length us, event | category | flops | bytes accessed | tf_op | source)
XLA Modules:
  0.0 76.2 jit_solution(15256095154108352722)
XLA Ops:
  7.2 0.0 all-gather.9.cloned.1.call-start
  7.2 0.7 all-gather.9.cloned.1.call-update
  7.9 12.7 %all-gather.3 = s32[1,512,1]{1,2,0:T(1,128)S(1)} all-gather(s32[1,128,1]{1,2,0:T(1,128)} %param.8), channel_id=5, replica_groups=mesh['group'=2,'row'=4,'cent'=4] {'row'}, dimensions={1}, use_global_device_ids=true | all-gather | bytes 2560 | tf_op jit(solution)/shard_map/all_gather | solution.py:54
  20.6 7.8 %all-gather.2 = s32[1,512]{1,0:T(1,128)S(1)} all-gather(s32[1,128]{1,0:T(1,128)} %param.9), channel_id=4, replica_groups=mesh['group'=2,'row'=4,'cent'=4] {'row'}, dimensions={1}, use_global_device_ids=true | all-gather | bytes 2560 | tf_op jit(solution)/shard_map/all_gather | solution.py:55
  28.5 0.3 convert_reduce_fusion
  28.7 1.5 %fusion = f32[512]{0:T(512)S(1)} fusion(bf16[1,512,1024]{2,1,0:T(8,128)(2,1)} %param.7), kind=kLoop, calls=%fused_computation.4 | loop fusion | flops 1572352 | bytes 1050624 | tf_op jit(solution)/shard_map/reduce_sum | solution.py:51
  30.3 0.0 copy-start
  30.3 10.0 %all-gather.9.cloned.1.call-done = bf16[1,512,1024]{2,1,0:T(8,128)(2,1)} async-done(((bf16[1,128,1024]{2,1,0:T(8,128)(2,1)}), bf16[1,512,1024]{2,1,0:T(8,128)(2,1)}) %all-gather.9.cloned.1.call-update) | async-done | bytes 1048592 | tf_op jit(solution)/shard_map/all_gather | solution.py:53
  40.2 0.0 copy-start.1
  40.2 2.5 %select_reduce_fusion = (f32[512]{0:T(512)S(1)}, f32[512]{0:T(512)S(1)}) fusion(s32[512]{0:T(512)S(1)} %bitcast.42, pred[512]{0:T(512)(128)(4,1)S(1)} %compare_reduce_fusion, f32[512]{0:T(512)S(1)} %broadcast_multiply_fusion, bf16[1,512,1024]{2,1,0:T(8,128)(2,1)} %param.7, bf16[1,512,1024]{2,1,0:T(8,128)(2,1)} %all-gather.9.cloned.1.call-done), kind=kOutput, calls=%fused_computation.13 | convolution fusion | flops 538442752 | bytes 2105856 | tf_op jit(solution)/shard_map/dot_general | solution.py:19
  42.7 11.9 %all-gather.5 = f32[4,1,512]{2,1,0:T(1,128)S(1)} all-gather(f32[1,1,512]{2,1,0:T(1,128)S(1)} %bitcast.45), channel_id=3, replica_groups=mesh['group'=2,'row'=4,'cent'=4] {'row'}, dimensions={0}, use_global_device_ids=true | all-gather | bytes 10240 | tf_op jit(solution)/shard_map/all_gather | solution.py:8
  54.6 11.9 %all-gather.6 = f32[4,1,512]{2,1,0:T(1,128)S(1)} all-gather(f32[1,1,512]{2,1,0:T(1,128)S(1)} %bitcast.44), channel_id=6, replica_groups=mesh['group'=2,'row'=4,'cent'=4] {'row'}, dimensions={0}, use_global_device_ids=true | all-gather | bytes 10240 | tf_op jit(solution)/shard_map/all_gather | solution.py:8
  66.5 0.2 while.17
  66.7 0.6 subtract_bitcast_fusion
  67.3 0.0 copy-done
  67.3 0.0 copy-done.1
  67.3 2.1 %fusion.2 = f32[1,512,1024]{2,1,0:T(8,128)} fusion(bf16[1,512,1024]{2,1,0:T(8,128)(2,1)S(1)} %copy-done, bf16[1,512,1024]{2,1,0:T(8,128)(2,1)S(1)} %copy-done.1, f32[512]{0:T(512)S(1)} %broadcast_add_fusion, s32[512]{0:T(512)S(1)} %bitcast.43, pred[512]{0:T(512)(128)(4,1)S(1)} %compare_reduce_fusion), kind=kOutput, calls=%fused_computation.6 | convolution fusion | flops 538968064 | bytes 4198912 | tf_op jit(solution)/shard_map/dot_general | solution.py:34
  (16 shorter events, 0.1 us)
Async XLA Ops:
  7.2 33.1 %all-gather.9.cloned.1.call-start = ((), (), s32[]{:S(2)}) async-start(), calls=%async_computation | async-start | bytes 1310720 | tf_op jit(solution)/shard_map/all_gather | solution.py:53
  30.3 37.0 %copy-start = (bf16[1,512,1024]{2,1,0:T(8,128)(2,1)S(1)}, bf16[1,512,1024]{2,1,0:T(8,128)(2,1)}, u32[]{:S(2)}) copy-start(bf16[1,512,1024]{2,1,0:T(8,128)(2,1)} %param.7) | copy-start | bytes 3145732
  40.2 27.0 %copy-start.1 = (bf16[1,512,1024]{2,1,0:T(8,128)(2,1)S(1)}, bf16[1,512,1024]{2,1,0:T(8,128)(2,1)}, u32[]{:S(2)}) copy-start(bf16[1,512,1024]{2,1,0:T(8,128)(2,1)} %all-gather.9.cloned.1.call-done) | copy-start | bytes 3145732
Sparse Core Ops, SparseCore 0:
  9.6 30.6 all-gather.8
where the time goes:
time: 76.4 us; the launch traced here: 76.2 us
  blocking collectives  44.3 us (58%)
  between operations  14.1 us (18%)
  waiting for transfers between devices  10.6 us (14%)
  matrix products  4.55 us (6%)
  other arithmetic  2.45 us (3%)
    all_gather x2, blocking collectives, combined_all(): gathered = jax.tree.map(lambda a: lax.all_gather(a, axis), part)  23.7 us
    all_gather x1, blocking collectives, body(): lax.all_gather(owner_ids, 'row', axis=0, tiled=True)  12.7 us
    all_gather x1, waiting for transfers between devices, body(): lax.all_gather(embed_rows, 'row', axis=0, tiled=True)  9.96 us
    all_gather x1, blocking collectives, body(): lax.all_gather(slot_ids, 'row', axis=0, tiled=True)  7.85 us
    dot_general x1, matrix products, score_piece(): lax.dot_general(piece_rows, cent_block, (((1,), (1,)), ((), ())), preferr...  2.49 us
    dot_general x1, matrix products, member_sums(): jnp.dot(member.astype(jnp.bfloat16), piece_rows, preferred_element_type=j...  2.06 us
  transfers between devices with their start and end apart: 1, of which 1 were waited for; matrix products, arithmetic and copies ran while one was open for 2% of the time, Pallas kernels for 0%

commit v1 on v0

v1 whole, which is shorter than its diff:
```python
import functools
import jax
import jax.numpy as jnp
from jax import lax
from jax.experimental import pallas as pl
from jax.experimental.pallas import tpu as pltpu
from jax.sharding import PartitionSpec as P

MESH = pl.DeviceIdType.MESH
PARTS = 4
NT = (((1,), (1,)), ((), ()))


def kernel(
    n, emb, cent_hbm, owner_hbm, slot_hbm, gap_out, new_out,
    owner, slot, rows, cent, acc, ids, idrow, hn, rcp, res_out, res_in,
    recv, send_l, send_r, id_recv, id_send, res_recv, res_send, local,
):
    z = lax.axis_index("row")
    count = emb.shape[0]
    k_dev = cent.shape[0]
    rc = count // PARTS
    groups = n // PARTS

    def remote(src, dst, s_sem, r_sem, target):
        return pltpu.make_async_remote_copy(
            src_ref=src, dst_ref=dst, send_sem=s_sem, recv_sem=r_sem,
            device_id={"row": target}, device_id_type=MESH,
        )

    def place(b, c):
        return rows.at[pl.ds(pl.multiple_of((c * n + b) * rc, rc), rc)]

    def own_src(c):
        return emb.at[pl.ds(c * rc, rc)]

    def own_left(c):
        return remote(own_src(c), place(z, c), send_l.at[z, c], recv.at[z, c], z - 1)

    def own_right(c):
        return remote(own_src(c), place(z, c), send_r.at[z, c], recv.at[z, c], z + 1)

    def pass_left(b, c):
        return remote(place(b, c), place(b, c), send_l.at[b, c], recv.at[b, c], z - 1)

    def pass_right(b, c):
        return remote(place(b, c), place(b, c), send_r.at[b, c], recv.at[b, c], z + 1)

    def each_other(fn):
        if n <= 4:
            for o in range(1, n):
                fn(lax.rem(z + o, n))
        else:
            def step(o, carry):
                fn(lax.rem(z + o, n))
                return carry
            lax.fori_loop(1, n, step, 0)

    barrier = pltpu.get_barrier_semaphore()
    each_other(
        lambda t: pl.semaphore_signal(barrier, inc=1, device_id={"row": t}, device_id_type=MESH)
    )
    id_copies = [
        pltpu.make_async_copy(owner_hbm, owner, local.at[PARTS + 1]),
        pltpu.make_async_copy(slot_hbm, slot, local.at[PARTS + 2]),
    ]
    for copy in id_copies:
        copy.start()
    cent_copy = pltpu.make_async_copy(cent_hbm, cent, local.at[0])
    cent_copy.start()
    own_copies = [
        pltpu.make_async_copy(own_src(c), place(z, c), local.at[1 + c]) for c in range(PARTS)
    ]
    for copy in own_copies:
        copy.start()
    for copy in id_copies:
        copy.wait()
    ids[z] = owner[...] * k_dev + slot[...]
    pl.semaphore_wait(barrier, n - 1)

    for c in range(PARTS):
        @pl.when(z > 0)
        def _():
            own_left(c).start()

        @pl.when(z < n - 1)
        def _():
            own_right(c).start()

        if c == 0:
            each_other(
                lambda t: remote(ids.at[z], ids.at[z], id_send.at[t], id_recv.at[z], t).start()
            )

    cent_copy.wait()
    tile = min(128, k_dev)
    for k in range(0, k_dev, tile):
        block = cent[pl.ds(k, tile), :].astype(jnp.float32)
        hn[pl.ds(k, tile), :] = 0.5 * jnp.sum(block * block, axis=1, keepdims=True)
        acc[pl.ds(k, tile), :] = block
    for copy in own_copies:
        copy.wait()

    each_other(lambda t: remote(ids.at[z], ids.at[z], id_send.at[t], id_recv.at[t], t).wait_recv())
    lane_block = lax.broadcasted_iota(jnp.int32, (1, count), 1) // rc
    cent_ids = lax.broadcasted_iota(jnp.int32, (k_dev, count), 0)
    found = jnp.zeros((k_dev, count), jnp.float32)
    for g in range(groups):
        mine = [ids[g * PARTS + j] - z * k_dev for j in range(PARTS)]
        for c in range(PARTS):
            row = jnp.zeros((1, count), jnp.int32)
            for j in range(PARTS):
                shift = ((j - c) * rc) % count
                moved = mine[j] if shift == 0 else pltpu.roll(mine[j], shift, 1)
                row = jnp.where(lane_block == j, moved, row)
            idrow[g * PARTS + c] = row
            found = found + jnp.where(cent_ids == row, 1.0, 0.0)
    rcp[...] = 1.0 / (1.0 + jnp.sum(found, axis=1, keepdims=True))

    def gather_round(c):
        def step(s, carry):
            @pl.when(z + s < n)
            def _():
                pass_left(z + s, c).wait_recv()

                @pl.when(z > 0)
                def _():
                    pass_left(z + s, c).start()

            @pl.when(z - s >= 0)
            def _():
                pass_right(z - s, c).wait_recv()

                @pl.when(z < n - 1)
                def _():
                    pass_right(z - s, c).start()

            return carry

        lax.fori_loop(1, n, step, 0)

    def block_of(c, g):
        return rows[pl.ds(pl.multiple_of((c * n + g * PARTS) * rc, count), count), :]

    def over_groups(fn):
        if groups == 1:
            fn(0)
        else:
            def step(g, carry):
                fn(g)
                return carry
            lax.fori_loop(0, groups, step, 0)

    def score(c, g):
        scores = lax.dot_general(cent[...], block_of(c, g), NT, preferred_element_type=jnp.float32)
        scores = scores - hn[...]
        member = cent_ids == idrow[g * PARTS + c]
        res_out[g, pl.ds(c, 1), :] = jnp.max(scores, axis=0, keepdims=True)
        res_out[g, pl.ds(PARTS + c, 1), :] = jnp.sum(
            jnp.where(member, scores, 0.0), axis=0, keepdims=True
        )

    def sums(c, g, k):
        member = cent_ids[k:k + tile] == idrow[g * PARTS + c]
        return jnp.dot(
            jnp.where(member, 1.0, 0.0).astype(jnp.bfloat16), block_of(c, g),
            preferred_element_type=jnp.float32,
        )

    def add_sums(c, g):
        for k in range(0, k_dev, tile):
            acc[pl.ds(k, tile), :] += sums(c, g, k)

    for c in range(PARTS):
        gather_round(c)
        over_groups(functools.partial(score, c))
        if c < PARTS - 1:
            over_groups(functools.partial(add_sums, c))

    each_other(
        lambda t: remote(
            res_out.at[t // PARTS], res_in.at[z], res_send.at[t], res_recv.at[z], t
        ).start()
    )
    res_in[z] = res_out[z // PARTS]
    last = PARTS - 1
    if groups > 1:
        def step(g, carry):
            add_sums(last, g)
            return carry
        lax.fori_loop(0, groups - 1, step, 0)
    for k in range(0, k_dev, tile):
        total = acc[pl.ds(k, tile), :] + sums(last, groups - 1, k)
        new_out[pl.ds(k, tile), :] = total * rcp[pl.ds(k, tile), :]

    def wait_sends(c):
        def step(s, carry):
            @pl.when((z + s < n) & (z > 0))
            def _():
                pass_left(z + s, c).wait_send()

            @pl.when((z - s >= 0) & (z < n - 1))
            def _():
                pass_right(z - s, c).wait_send()

            return carry

        lax.fori_loop(0, n, step, 0)

    for c in range(PARTS):
        wait_sends(c)
    each_other(lambda t: remote(ids.at[z], ids.at[z], id_send.at[t], id_recv.at[t], t).wait_send())
    each_other(
        lambda t: remote(
            res_out.at[t // PARTS], res_in.at[t], res_send.at[t], res_recv.at[t], t
        ).wait()
    )
    got = res_in[...]
    best = jnp.max(got, axis=0)
    chosen = jnp.sum(got, axis=0)
    gap = best[0:PARTS] - chosen[PARTS:2 * PARTS]
    gap = pltpu.roll(gap, lax.rem((PARTS - lax.rem(z, PARTS)) * rc, count), 1)
    line = jnp.zeros((1, count), jnp.float32)
    for c in range(PARTS):
        moved = gap[c:c + 1] if c == 0 else pltpu.roll(gap[c:c + 1], c * rc, 1)
        line = jnp.where(lane_block == c, moved, line)
    gap_out[...] = line


def body(embeddings, centroids, owner, slot):
    n = lax.axis_size("row")
    count, width = embeddings.shape[1:]
    k_dev = centroids.shape[1]
    groups = n // PARTS
    vmem = pl.BlockSpec(memory_space=pltpu.VMEM)
    hbm = pl.BlockSpec(memory_space=pltpu.HBM)
    dma = pltpu.SemaphoreType.DMA
    gap, updated = pl.pallas_call(
        functools.partial(kernel, n),
        out_shape=(
            jax.ShapeDtypeStruct((1, count), jnp.float32),
            jax.ShapeDtypeStruct((k_dev, width), jnp.float32),
        ),
        in_specs=[hbm, hbm, hbm, hbm],
        out_specs=(vmem, vmem),
        scratch_shapes=[
            pltpu.VMEM((1, count), jnp.int32),
            pltpu.VMEM((1, count), jnp.int32),
            pltpu.VMEM((n * count, width), jnp.bfloat16),
            pltpu.VMEM((k_dev, width), jnp.bfloat16),
            pltpu.VMEM((k_dev, width), jnp.float32),
            pltpu.VMEM((n, 1, count), jnp.int32),
            pltpu.VMEM((n, 1, count), jnp.int32),
            pltpu.VMEM((k_dev, 1), jnp.float32),
            pltpu.VMEM((k_dev, 1), jnp.float32),
            pltpu.VMEM((groups, 2 * PARTS, count), jnp.float32),
            pltpu.VMEM((n, 2 * PARTS, count), jnp.float32),
            dma((n, PARTS)),
            dma((n, PARTS)),
            dma((n, PARTS)),
            dma((n,)),
            dma((n,)),
            dma((n,)),
            dma((n,)),
            dma((3 + PARTS,)),
        ],
        compiler_params=pltpu.CompilerParams(
            collective_id=0, has_side_effects=True, vmem_limit_bytes=40 * 2**20
        ),
    )(embeddings[0], centroids[0], owner[:, :, 0], slot)
    return gap, updated[None]


def solution(mesh):
    placed = (
        P(("group", "cent"), "row", None),
        P(("group", "cent"), "row", None),
        P(("group", "cent"), "row", None),
        P(("group", "cent"), "row"),
    )
    return jax.shard_map(
        body,
        mesh=mesh,
        in_specs=placed,
        out_specs=(P(("group", "cent"), "row"), P(("group", "cent"), "row", None)),
        check_vma=False,
    )
```

time: 76.4 us -> 39.5 us (0.52)
  blocking collectives: 44.3 us -> 0 us
  Pallas kernels: 0 us -> 33.3 us
  between operations: 14.1 us -> 0.65 us
  waiting for transfers between devices: 10.6 us -> 0 us
  local copies, waits for them, and re-layouts: 0.05 us -> 5.31 us
  matrix products: 4.55 us -> 0 us
  other arithmetic: 2.45 us -> 0 us
    all_gather x4 -> x0, blocking collectives: 44.3 us -> none  [the longest x2 23.7 us: combined_all(): gathered = jax.tree.map(lambda a: lax.all_gather(a, axis), part)]
    pallas_call x0 -> x1, Pallas kernels: none -> 33.3 us  [body(): pl.pallas_call(functools.partial(kernel, n), out_shape=(jax.ShapeDtypeStr...]
    all_gather x1 -> x0, waiting for transfers between devices: 9.96 us -> none  [body(): lax.all_gather(embed_rows, 'row', axis=0, tiled=True)]
    unnamed x6 -> x10, local copies, waits for them, and re-layouts: 0.02 us -> 5.31 us
    dot_general x2 -> x0, matrix products: 4.55 us -> none  [the longest x1 2.49 us: score_piece(): lax.dot_general(piece_rows, cent_block, (((1,), (1,)), ((), ())), preferr...]
    reduce_sum x2 -> x0, other arithmetic: 1.76 us -> none  [the longest x1 1.51 us: body(): jnp.sum(jnp.square(cent_block.astype(jnp.float32)), axis=1)]
  transfers between devices with their start and end apart: 1 -> 0, of which waited for: 1 -> 0; matrix products, arithmetic and copies ran while one was open for 2% -> 0% of each run, Pallas kernels for 0% -> 0%
where the time goes in v1:
time: 39.5 us; the launch traced here: 39.3 us
  Pallas kernels  33.3 us (84%)
  local copies, waits for them, and re-layouts  5.31 us (13%)
  between operations  0.65 us (2%)
    pallas_call x1, Pallas kernels, body(): pl.pallas_call(functools.partial(kernel, n), out_shape=(jax.ShapeDtypeStr...  33.3 us
    unnamed x10, local copies, waits for them, and re-layouts  5.31 us

profile of v1, /device:TPU:0, one launch (start us, length us, event | category | flops | bytes accessed | tf_op | source)
XLA Modules:
  0.0 39.3 jit_solution(2448152251069770948)
XLA Ops:
  0.6 0.0 copy-start
  0.6 1.2 %copy-done = bf16[1,512,1024]{2,1,0:T(8,128)(2,1)S(1)} copy-done((bf16[1,512,1024]{2,1,0:T(8,128)(2,1)S(1)}, bf16[1,512,1024]{2,1,0:T(8,128)(2,1)}, u32[]{:S(2)}) %copy-start) | copy-done | bytes 1048600
  1.9 0.0 copy-start.1
  1.9 0.9 %copy-done.1 = bf16[1,128,1024]{2,1,0:T(8,128)(2,1)S(1)} copy-done((bf16[1,128,1024]{2,1,0:T(8,128)(2,1)S(1)}, bf16[1,128,1024]{2,1,0:T(8,128)(2,1)}, u32[]{:S(2)}) %copy-start.1) | copy-done | bytes 262168
  2.8 0.0 copy-start.2
  2.8 0.7 %copy-done.2 = s32[1,128,1]{1,2,0:T(1,128)S(1)} copy-done((s32[1,128,1]{1,2,0:T(1,128)S(1)}, s32[1,128,1]{1,2,0:T(1,128)}, u32[]{:S(2)}) %copy-start.2) | copy-done | bytes 536
  3.5 0.0 copy-start.3
  3.5 0.7 %copy-done.3 = s32[1,128]{1,0:T(1,128)S(1)} copy-done((s32[1,128]{1,0:T(1,128)S(1)}, s32[1,128]{1,0:T(1,128)}, u32[]{:S(2)}) %copy-start.3) | copy-done | bytes 536
  4.1 33.3 %shard_map.59 = (f32[1,128]{1,0:T(1,128)S(1)}, f32[512,1024]{1,0:T(8,128)S(1)}) custom-call(bf16[128,1024]{1,0:T(8,128)(2,1)S(1)} %bitcast.6, bf16[512,1024]{1,0:T(8,128)(2,1)S(1)} %bitcast.5, s32[1,128]{1,0:T(1,128)S(1)} %bitcast.7, s32[1,128]{1,0:T(1,128)S(1)} %copy-done.3), custom_call_target="tpu_custom_call" | custom-call | tf_op jit(solution)/shard_map/pallas_call | solution.py:238
  37.4 0.5 %copy.8 = f32[1,128]{1,0:T(1,128)} copy(f32[1,128]{1,0:T(1,128)S(1)} %get-tuple-element.8) | data formatting | bytes 1024
  38.0 1.3 %copy.9 = f32[1,512,1024]{2,1,0:T(8,128)} copy(f32[1,512,1024]{2,1,0:T(8,128)S(1)} %bitcast.4) | data formatting | bytes 4194304
Async XLA Ops:
  0.6 1.2 %copy-start = (bf16[1,512,1024]{2,1,0:T(8,128)(2,1)S(1)}, bf16[1,512,1024]{2,1,0:T(8,128)(2,1)}, u32[]{:S(2)}) copy-start(bf16[1,512,1024]{2,1,0:T(8,128)(2,1)} %param.5) | copy-start | bytes 3145732
  1.9 0.9 %copy-start.1 = (bf16[1,128,1024]{2,1,0:T(8,128)(2,1)S(1)}, bf16[1,128,1024]{2,1,0:T(8,128)(2,1)}, u32[]{:S(2)}) copy-start(bf16[1,128,1024]{2,1,0:T(8,128)(2,1)} %param.4) | copy-start | bytes 786436
  2.8 0.7 %copy-start.2 = (s32[1,128,1]{1,2,0:T(1,128)S(1)}, s32[1,128,1]{1,2,0:T(1,128)}, u32[]{:S(2)}) copy-start(s32[1,128,1]{1,2,0:T(1,128)} %param.6) | copy-start | bytes 1540
  3.5 0.7 %copy-start.3 = (s32[1,128]{1,0:T(1,128)S(1)}, s32[1,128]{1,0:T(1,128)}, u32[]{:S(2)}) copy-start(s32[1,128]{1,0:T(1,128)} %slot_hbm.1) | copy-start | bytes 1540

commit v2 on v1

v2 whole, which is shorter than its diff:
```python
import functools
import jax
import jax.numpy as jnp
from jax import lax
from jax.experimental import pallas as pl
from jax.experimental.pallas import tpu as pltpu
from jax.sharding import PartitionSpec as P

MESH = pl.DeviceIdType.MESH
PARTS = 4
NT = (((1,), (1,)), ((), ()))


def kernel(
    n, emb, cent_hbm, owner_hbm, slot_hbm, gap_out, new_out,
    owner, slot, rows, cent, ids, hn, rcp, res_out, res_in,
    recv, send_l, send_r, id_recv, id_send, res_recv, res_send, local,
):
    z = lax.axis_index("row")
    count = emb.shape[0]
    k_dev = cent.shape[0]
    rc = count // PARTS

    def remote(src, dst, s_sem, r_sem, target):
        return pltpu.make_async_remote_copy(
            src_ref=src, dst_ref=dst, send_sem=s_sem, recv_sem=r_sem,
            device_id={"row": target}, device_id_type=MESH,
        )

    def place(b, c):
        return rows.at[b, pl.ds(c * rc, rc)]

    def own_src(c):
        return emb.at[pl.ds(c * rc, rc)]

    def own_left(c):
        return remote(own_src(c), place(z, c), send_l.at[z, c], recv.at[z, c], z - 1)

    def own_right(c):
        return remote(own_src(c), place(z, c), send_r.at[z, c], recv.at[z, c], z + 1)

    def pass_left(b, c):
        return remote(place(b, c), place(b, c), send_l.at[b, c], recv.at[b, c], z - 1)

    def pass_right(b, c):
        return remote(place(b, c), place(b, c), send_r.at[b, c], recv.at[b, c], z + 1)

    def each_other(fn):
        if n <= 4:
            for o in range(1, n):
                fn(lax.rem(z + o, n))
        else:
            def step(o, carry):
                fn(lax.rem(z + o, n))
                return carry
            lax.fori_loop(1, n, step, 0)

    barrier = pltpu.get_barrier_semaphore()
    each_other(
        lambda t: pl.semaphore_signal(barrier, inc=1, device_id={"row": t}, device_id_type=MESH)
    )
    id_copies = [
        pltpu.make_async_copy(owner_hbm, owner, local.at[PARTS + 1]),
        pltpu.make_async_copy(slot_hbm, slot, local.at[PARTS + 2]),
    ]
    for copy in id_copies:
        copy.start()
    cent_copy = pltpu.make_async_copy(cent_hbm, cent, local.at[0])
    cent_copy.start()
    own_copies = [
        pltpu.make_async_copy(own_src(c), place(z, c), local.at[1 + c]) for c in range(PARTS)
    ]
    for copy in own_copies:
        copy.start()
    for copy in id_copies:
        copy.wait()
    ids[z] = owner[...] * k_dev + slot[...]
    pl.semaphore_wait(barrier, n - 1)

    for c in range(PARTS):
        @pl.when(z > 0)
        def _():
            own_left(c).start()

        @pl.when(z < n - 1)
        def _():
            own_right(c).start()

        if c == 0:
            each_other(
                lambda t: remote(ids.at[z], ids.at[z], id_send.at[t], id_recv.at[z], t).start()
            )

    cent_copy.wait()
    tile = min(128, k_dev)
    for k in range(0, k_dev, tile):
        block = cent[pl.ds(k, tile), :].astype(jnp.float32)
        hn[pl.ds(k, tile), :] = 0.5 * jnp.sum(block * block, axis=1, keepdims=True)
    for copy in own_copies:
        copy.wait()

    cent_ids = lax.broadcasted_iota(jnp.int32, (k_dev, count), 0)

    def member_of(b):
        return cent_ids == ids[b] - z * k_dev

    def score(b):
        scores = lax.dot_general(cent[...], rows[b], NT, preferred_element_type=jnp.float32)
        scores = scores - hn[...]
        best = jnp.max(scores, axis=0, keepdims=True)
        chosen = jnp.sum(jnp.where(member_of(b), scores, 0.0), axis=0, keepdims=True)
        return best, chosen

    def add_sums(b, first=False):
        member = jnp.where(member_of(b), 1.0, 0.0).astype(jnp.bfloat16)
        for k in range(0, k_dev, tile):
            part = jnp.dot(member[k:k + tile], rows[b], preferred_element_type=jnp.float32)
            here = pl.ds(k, tile)
            if first:
                new_out[here, :] = (cent[here, :].astype(jnp.float32) + part) * rcp[here, :]
            else:
                new_out[here, :] += part * rcp[here, :]

    def result(b):
        return remote(res_out.at[b], res_in.at[z], res_send.at[b], res_recv.at[z], b)

    def answer(b):
        best, chosen = score(b)
        res_out[b, 0:1, :] = best
        res_out[b, 1:2, :] = chosen
        result(b).start()

    each_other(lambda t: remote(ids.at[z], ids.at[z], id_send.at[t], id_recv.at[t], t).wait_recv())
    best, chosen = score(z)
    res_in[z, 0:1, :] = best
    res_in[z, 1:2, :] = chosen
    if n <= 4:
        found = sum(jnp.where(member_of(b), 1.0, 0.0) for b in range(n))
    else:
        found = lax.fori_loop(
            0, n, lambda b, f: f + jnp.where(member_of(b), 1.0, 0.0),
            jnp.zeros((k_dev, count), jnp.float32),
        )
    rcp[...] = 1.0 / (1.0 + jnp.sum(found, axis=1, keepdims=True))
    add_sums(z, True)

    def step(s, carry):
        for c in range(PARTS):
            @pl.when(z + s < n)
            def _():
                pass_left(z + s, c).wait_recv()

                @pl.when(z > 0)
                def _():
                    pass_left(z + s, c).start()

            @pl.when(z - s >= 0)
            def _():
                pass_right(z - s, c).wait_recv()

                @pl.when(z < n - 1)
                def _():
                    pass_right(z - s, c).start()

        @pl.when(z + s < n)
        def _():
            answer(z + s)

        @pl.when(z - s >= 0)
        def _():
            answer(z - s)

        @pl.when(z + s < n)
        def _():
            add_sums(z + s)

        @pl.when(z - s >= 0)
        def _():
            add_sums(z - s)

        return carry

    lax.fori_loop(1, n, step, 0)

    def wait_sends(s, carry):
        for c in range(PARTS):
            @pl.when((z + s < n) & (z > 0))
            def _():
                pass_left(z + s, c).wait_send()

            @pl.when((z - s >= 0) & (z < n - 1))
            def _():
                pass_right(z - s, c).wait_send()

        return carry

    lax.fori_loop(0, n, wait_sends, 0)
    each_other(lambda t: remote(ids.at[z], ids.at[z], id_send.at[t], id_recv.at[t], t).wait_send())
    each_other(
        lambda t: remote(res_out.at[t], res_in.at[t], res_send.at[t], res_recv.at[t], t).wait()
    )
    got = res_in[...]
    gap_out[...] = jnp.max(got[:, 0], axis=0, keepdims=True) - jnp.sum(got[:, 1], axis=0, keepdims=True)


def body(embeddings, centroids, owner, slot):
    n = lax.axis_size("row")
    count, width = embeddings.shape[1:]
    k_dev = centroids.shape[1]
    vmem = pl.BlockSpec(memory_space=pltpu.VMEM)
    hbm = pl.BlockSpec(memory_space=pltpu.HBM)
    dma = pltpu.SemaphoreType.DMA
    gap, updated = pl.pallas_call(
        functools.partial(kernel, n),
        out_shape=(
            jax.ShapeDtypeStruct((1, count), jnp.float32),
            jax.ShapeDtypeStruct((k_dev, width), jnp.float32),
        ),
        in_specs=[hbm, hbm, hbm, hbm],
        out_specs=(vmem, vmem),
        scratch_shapes=[
            pltpu.VMEM((1, count), jnp.int32),
            pltpu.VMEM((1, count), jnp.int32),
            pltpu.VMEM((n, count, width), jnp.bfloat16),
            pltpu.VMEM((k_dev, width), jnp.bfloat16),
            pltpu.VMEM((n, 1, count), jnp.int32),
            pltpu.VMEM((k_dev, 1), jnp.float32),
            pltpu.VMEM((k_dev, 1), jnp.float32),
            pltpu.VMEM((n, 2, count), jnp.float32),
            pltpu.VMEM((n, 2, count), jnp.float32),
            dma((n, PARTS)),
            dma((n, PARTS)),
            dma((n, PARTS)),
            dma((n,)),
            dma((n,)),
            dma((n,)),
            dma((n,)),
            dma((3 + PARTS,)),
        ],
        compiler_params=pltpu.CompilerParams(
            collective_id=0, has_side_effects=True, vmem_limit_bytes=56 * 2**20
        ),
    )(embeddings[0], centroids[0], owner[:, :, 0], slot)
    return gap, updated[None]


def solution(mesh):
    placed = (
        P(("group", "cent"), "row", None),
        P(("group", "cent"), "row", None),
        P(("group", "cent"), "row", None),
        P(("group", "cent"), "row"),
    )
    return jax.shard_map(
        body,
        mesh=mesh,
        in_specs=placed,
        out_specs=(P(("group", "cent"), "row"), P(("group", "cent"), "row", None)),
        check_vma=False,
    )
```

time: 39.5 us -> 33.8 us (0.86)
  Pallas kernels: 33.3 us -> 28.7 us
  local copies, waits for them, and re-layouts: 5.31 us -> 4.3 us
    pallas_call x1, Pallas kernels: 33.3 us -> 28.7 us  [body(): pl.pallas_call(functools.partial(kernel, n), out_shape=(jax.ShapeDtypeStr...]
    unnamed x10 -> x2, local copies, waits for them, and re-layouts: 5.31 us -> 4.3 us
where the time goes in v2:
time: 33.8 us; the launch traced here: 33.6 us
  Pallas kernels  28.7 us (85%)
  local copies, waits for them, and re-layouts  4.3 us (13%)
  between operations  0.64 us (2%)
    pallas_call x1, Pallas kernels, body(): pl.pallas_call(functools.partial(kernel, n), out_shape=(jax.ShapeDtypeStr...  28.7 us
    unnamed x2, local copies, waits for them, and re-layouts  4.3 us

profile of v2, /device:TPU:0, one launch (start us, length us, event | category | flops | bytes accessed | tf_op | source)
XLA Modules:
  0.0 33.6 jit_solution(2583831914849833893)
XLA Ops:
  0.6 28.7 %shard_map.59 = (f32[1,128]{1,0:T(1,128)}, f32[512,1024]{1,0:T(8,128)}) custom-call(bf16[128,1024]{1,0:T(8,128)(2,1)} %bitcast.6, bf16[512,1024]{1,0:T(8,128)(2,1)} %bitcast.5, s32[1,128]{1,0:T(1,128)} %bitcast.7, s32[1,128]{1,0:T(1,128)} %slot_hbm.1), custom_call_target="tpu_custom_call" | custom-call | tf_op jit(solution)/shard_map/pallas_call | solution.py:213
  29.3 1.1 %copy.8 = f32[1,128]{1,0:T(1,128)} copy(f32[1,128]{1,0:T(1,128)} %get-tuple-element.8) | data formatting | bytes 1024
  30.5 3.2 %copy.9 = f32[1,512,1024]{2,1,0:T(8,128)} copy(f32[1,512,1024]{2,1,0:T(8,128)} %bitcast.4) | data formatting | bytes 4194304

commit v3 on v2

--- a/solution.py
+++ b/solution.py
@@ -12,9 +12,9 @@
 
 
 def kernel(
-    n, emb, cent_hbm, owner_hbm, slot_hbm, gap_out, new_out,
-    owner, slot, rows, cent, ids, hn, rcp, res_out, res_in,
-    recv, send_l, send_r, id_recv, id_send, res_recv, res_send, local,
+    n, emb, cent_hbm, owner_hbm, slot_hbm, gap_out, rows_out, ids_out,
+    owner, slot, rows, cent, ids, hn, res_out, res_in,
+    recv, send_l, send_r, id_recv, id_send, res_recv, res_send, out_sem, local,
 ):
     z = lax.axis_index("row")
     count = emb.shape[0]
@@ -111,15 +111,8 @@
         chosen = jnp.sum(jnp.where(member_of(b), scores, 0.0), axis=0, keepdims=True)
         return best, chosen
 
-    def add_sums(b, first=False):
-        member = jnp.where(member_of(b), 1.0, 0.0).astype(jnp.bfloat16)
-        for k in range(0, k_dev, tile):
-            part = jnp.dot(member[k:k + tile], rows[b], preferred_element_type=jnp.float32)
-            here = pl.ds(k, tile)
-            if first:
-                new_out[here, :] = (cent[here, :].astype(jnp.float32) + part) * rcp[here, :]
-            else:
-                new_out[here, :] += part * rcp[here, :]
+    def keep(b):
+        return pltpu.make_async_copy(rows.at[b], rows_out.at[b], out_sem.at[b])
 
     def result(b):
         return remote(res_out.at[b], res_in.at[z], res_send.at[b], res_recv.at[z], b)
@@ -134,15 +127,8 @@
     best, chosen = score(z)
     res_in[z, 0:1, :] = best
     res_in[z, 1:2, :] = chosen
-    if n <= 4:
-        found = sum(jnp.where(member_of(b), 1.0, 0.0) for b in range(n))
-    else:
-        found = lax.fori_loop(
-            0, n, lambda b, f: f + jnp.where(member_of(b), 1.0, 0.0),
-            jnp.zeros((k_dev, count), jnp.float32),
-        )
-    rcp[...] = 1.0 / (1.0 + jnp.sum(found, axis=1, keepdims=True))
-    add_sums(z, True)
+    keep(z).start()
+    ids_out[...] = ids[...] - z * k_dev
 
     def step(s, carry):
         for c in range(PARTS):
@@ -164,19 +150,13 @@
 
         @pl.when(z + s < n)
         def _():
+            keep(z + s).start()
             answer(z + s)
 
         @pl.when(z - s >= 0)
         def _():
+            keep(z - s).start()
             answer(z - s)
-
-        @pl.when(z + s < n)
-        def _():
-            add_sums(z + s)
-
-        @pl.when(z - s >= 0)
-        def _():
-            add_sums(z - s)
 
         return carry
 
@@ -199,25 +179,89 @@
     each_other(
         lambda t: remote(res_out.at[t], res_in.at[t], res_send.at[t], res_recv.at[t], t).wait()
     )
+    lax.fori_loop(0, n, lambda b, carry: (keep(b).wait(), carry)[1], 0)
     got = res_in[...]
     gap_out[...] = jnp.max(got[:, 0], axis=0, keepdims=True) - jnp.sum(got[:, 1], axis=0, keepdims=True)
+
+
+def finish(
+    n, rows_hbm, cent_hbm, ids_hbm, gap_hbm, gap_out, new_hbm,
+    rows, cent, ids, out, load, store, small,
+):
+    k_dev = cent.shape[0]
+    count = ids.shape[-1]
+    tile = min(128, k_dev)
+    tiles = range(0, k_dev, tile)
+    gap_copy = pltpu.make_async_copy(gap_hbm, gap_out, small.at[0])
+    ids_copy = pltpu.make_async_copy(ids_hbm, ids, small.at[1])
+    rows_copy = pltpu.make_async_copy(rows_hbm, rows, small.at[2])
+    ids_copy.start()
+    rows_copy.start()
+    gap_copy.start()
+    loads = [
+        pltpu.make_async_copy(cent_hbm.at[pl.ds(k, tile)], cent.at[pl.ds(k, tile)], load.at[i])
+        for i, k in enumerate(tiles)
+    ]
+    stores = [
+        pltpu.make_async_copy(out.at[pl.ds(k, tile)], new_hbm.at[pl.ds(k, tile)], store.at[i])
+        for i, k in enumerate(tiles)
+    ]
+    for copy in loads:
+        copy.start()
+    ids_copy.wait()
+    lanes = lax.broadcasted_iota(jnp.int32, (tile, count), 0)
+
+    def members(g, k):
+        return jnp.concatenate(
+            [
+                jnp.where(lanes + k == ids[g * PARTS + j], 1.0, 0.0)
+                for j in range(PARTS)
+            ],
+            axis=1,
+        )
+
+    def add(g, carry, k):
+        total, found = carry
+        member = members(g, k)
+        block = rows[pl.ds(g * PARTS, PARTS)].reshape(PARTS * count, rows.shape[-1])
+        total = total + jnp.dot(
+            member.astype(jnp.bfloat16), block, preferred_element_type=jnp.float32
+        )
+        return total, found + jnp.sum(member, axis=1, keepdims=True)
+
+    rows_copy.wait()
+    for i, k in enumerate(tiles):
+        loads[i].wait()
+        here = pl.ds(k, tile)
+        carry = (cent[here, :].astype(jnp.float32), jnp.ones((tile, 1), jnp.float32))
+        if n == PARTS:
+            total, found = add(0, carry, k)
+        else:
+            total, found = lax.fori_loop(0, n // PARTS, functools.partial(add, k=k), carry)
+        out[here, :] = total * (1.0 / found)
+        stores[i].start()
+    for copy in stores:
+        copy.wait()
+    gap_copy.wait()
 
 
 def body(embeddings, centroids, owner, slot):
     n = lax.axis_size("row")
     count, width = embeddings.shape[1:]
     k_dev = centroids.shape[1]
+    tiles = k_dev // min(128, k_dev)
     vmem = pl.BlockSpec(memory_space=pltpu.VMEM)
-    hbm = pl.BlockSpec(memory_space=pltpu.HBM)
+    hbm = pl.BlockSpec(memory_space=pl.ANY)
     dma = pltpu.SemaphoreType.DMA
-    gap, updated = pl.pallas_call(
+    gap, gathered, ids = pl.pallas_call(
         functools.partial(kernel, n),
         out_shape=(
             jax.ShapeDtypeStruct((1, count), jnp.float32),
-            jax.ShapeDtypeStruct((k_dev, width), jnp.float32),
+            jax.ShapeDtypeStruct((n, count, width), jnp.bfloat16),
+            jax.ShapeDtypeStruct((n, 1, count), jnp.int32),
         ),
         in_specs=[hbm, hbm, hbm, hbm],
-        out_specs=(vmem, vmem),
+        out_specs=(vmem, hbm, vmem),
         scratch_shapes=[
             pltpu.VMEM((1, count), jnp.int32),
             pltpu.VMEM((1, count), jnp.int32),
@@ -225,12 +269,12 @@
             pltpu.VMEM((k_dev, width), jnp.bfloat16),
             pltpu.VMEM((n, 1, count), jnp.int32),
             pltpu.VMEM((k_dev, 1), jnp.float32),
-            pltpu.VMEM((k_dev, 1), jnp.float32),
             pltpu.VMEM((n, 2, count), jnp.float32),
             pltpu.VMEM((n, 2, count), jnp.float32),
             dma((n, PARTS)),
             dma((n, PARTS)),
             dma((n, PARTS)),
+            dma((n,)),
             dma((n,)),
             dma((n,)),
             dma((n,)),
@@ -241,6 +285,25 @@
             collective_id=0, has_side_effects=True, vmem_limit_bytes=56 * 2**20
         ),
     )(embeddings[0], centroids[0], owner[:, :, 0], slot)
+    gap, updated = pl.pallas_call(
+        functools.partial(finish, n),
+        out_shape=(
+            jax.ShapeDtypeStruct((1, count), jnp.float32),
+            jax.ShapeDtypeStruct((k_dev, width), jnp.float32),
+        ),
+        in_specs=[hbm, hbm, hbm, hbm],
+        out_specs=(hbm, hbm),
+        scratch_shapes=[
+            pltpu.VMEM((n, count, width), jnp.bfloat16),
+            pltpu.VMEM((k_dev, width), jnp.bfloat16),
+            pltpu.VMEM((n, 1, count), jnp.int32),
+            pltpu.VMEM((k_dev, width), jnp.float32),
+            dma((tiles,)),
+            dma((tiles,)),
+            dma((3,)),
+        ],
+        compiler_params=pltpu.CompilerParams(vmem_limit_bytes=56 * 2**20),
+    )(gathered, centroids[0], ids, gap)
     return gap, updated[None]
 
 

time: 33.8 us -> 32.2 us (0.953)
  local copies, waits for them, and re-layouts: 4.3 us -> 0 us
  Pallas kernels: 28.7 us -> 31.4 us
    unnamed x2 -> x0, local copies, waits for them, and re-layouts: 4.3 us -> none
    pallas_call x0 -> x1, Pallas kernels: none -> 3.47 us  [body(): pl.pallas_call(functools.partial(finish, n), out_shape=(jax.ShapeDtypeStr...]
    pallas_call x1, Pallas kernels: 28.7 us -> 28 us  [body(): pl.pallas_call(functools.partial(kernel, n), out_shape=(jax.ShapeDtypeStr...]
where the time goes in v3:
time: 32.2 us; the launch traced here: 32.1 us
  Pallas kernels  31.4 us (98%)
  between operations  0.64 us (2%)
    pallas_call x1, Pallas kernels, body(): pl.pallas_call(functools.partial(kernel, n), out_shape=(jax.ShapeDtypeStr...  28 us
    pallas_call x1, Pallas kernels, body(): pl.pallas_call(functools.partial(finish, n), out_shape=(jax.ShapeDtypeStr...  3.47 us

profile of v3, /device:TPU:0, one launch (start us, length us, event | category | flops | bytes accessed | tf_op | source)
XLA Modules:
  0.0 32.1 jit_solution(14535781851600778684)
XLA Ops:
  0.6 28.0 %shard_map.59 = (f32[1,128]{1,0:T(1,128)}, bf16[4,128,1024]{2,1,0:T(8,128)(2,1)}, s32[4,1,128]{2,1,0:T(1,128)}) custom-call(bf16[128,1024]{1,0:T(8,128)(2,1)} %bitcast.6, bf16[512,1024]{1,0:T(8,128)(2,1)} %bitcast.4, s32[1,128]{1,0:T(1,128)} %bitcast.7, s32[1,128]{1,0:T(1,128)} %slot_hbm.1), custom_call_target="tpu_custom_call" | custom-call | tf_op jit(solution)/shard_map/pallas_call | solution.py:256
  28.6 3.5 %shard_map.60 = (f32[1,128]{1,0:T(1,128)}, f32[512,1024]{1,0:T(8,128)}) custom-call(bf16[4,128,1024]{2,1,0:T(8,128)(2,1)} %get-tuple-element.7.rows_hbm, bf16[512,1024]{1,0:T(8,128)(2,1)} %bitcast.5, s32[4,1,128]{2,1,0:T(1,128)} %get-tuple-element.8.ids_hbm, f32[1,128]{1,0:T(1,128)} %get-tuple-element.9.gap_hbm), custom_call_target="tpu_custom_call" | custom-call | tf_op jit(solution)/shard_map/pallas_call | solution.py:288

commit v4 on v3

--- a/solution.py
+++ b/solution.py
@@ -186,59 +186,47 @@
 
 def finish(
     n, rows_hbm, cent_hbm, ids_hbm, gap_hbm, gap_out, new_hbm,
-    rows, cent, ids, out, load, store, small,
+    rows, cent, ids, out, member, load_rows, load_cent, store, small,
 ):
-    k_dev = cent.shape[0]
+    tiles, k_dev, tile = cent.shape
     count = ids.shape[-1]
-    tile = min(128, k_dev)
-    tiles = range(0, k_dev, tile)
     gap_copy = pltpu.make_async_copy(gap_hbm, gap_out, small.at[0])
     ids_copy = pltpu.make_async_copy(ids_hbm, ids, small.at[1])
-    rows_copy = pltpu.make_async_copy(rows_hbm, rows, small.at[2])
     ids_copy.start()
-    rows_copy.start()
+    loads, stores = [], []
+    for i in range(tiles):
+        columns = pl.ds(i * tile, tile)
+        loads.append((
+            pltpu.make_async_copy(rows_hbm.at[:, :, columns], rows.at[i], load_rows.at[i]),
+            pltpu.make_async_copy(cent_hbm.at[:, columns], cent.at[i], load_cent.at[i]),
+        ))
+        stores.append(pltpu.make_async_copy(out.at[i], new_hbm.at[:, columns], store.at[i]))
+        for copy in loads[i]:
+            copy.start()
     gap_copy.start()
-    loads = [
-        pltpu.make_async_copy(cent_hbm.at[pl.ds(k, tile)], cent.at[pl.ds(k, tile)], load.at[i])
-        for i, k in enumerate(tiles)
-    ]
-    stores = [
-        pltpu.make_async_copy(out.at[pl.ds(k, tile)], new_hbm.at[pl.ds(k, tile)], store.at[i])
-        for i, k in enumerate(tiles)
-    ]
-    for copy in loads:
-        copy.start()
     ids_copy.wait()
-    lanes = lax.broadcasted_iota(jnp.int32, (tile, count), 0)
-
-    def members(g, k):
-        return jnp.concatenate(
-            [
-                jnp.where(lanes + k == ids[g * PARTS + j], 1.0, 0.0)
-                for j in range(PARTS)
-            ],
-            axis=1,
+    cent_ids = lax.broadcasted_iota(jnp.int32, (k_dev, count), 0)
+
+    def mark(b, found):
+        here = jnp.where(cent_ids == ids[b], 1.0, 0.0)
+        lanes = b * count if n <= 4 else pl.multiple_of(b * count, count)
+        member[:, pl.ds(lanes, count)] = here.astype(jnp.bfloat16)
+        return found + here
+
+    found = jnp.zeros((k_dev, count), jnp.float32)
+    if n <= 4:
+        for b in range(n):
+            found = mark(b, found)
+    else:
+        found = lax.fori_loop(0, n, mark, found)
+    rcp = 1.0 / (1.0 + jnp.sum(found, axis=1, keepdims=True))
+    for i in range(tiles):
+        for copy in loads[i]:
+            copy.wait()
+        total = cent[i].astype(jnp.float32) + jnp.dot(
+            member[...], rows[i].reshape(n * count, tile), preferred_element_type=jnp.float32
         )
-
-    def add(g, carry, k):
-        total, found = carry
-        member = members(g, k)
-        block = rows[pl.ds(g * PARTS, PARTS)].reshape(PARTS * count, rows.shape[-1])
-        total = total + jnp.dot(
-            member.astype(jnp.bfloat16), block, preferred_element_type=jnp.float32
-        )
-        return total, found + jnp.sum(member, axis=1, keepdims=True)
-
-    rows_copy.wait()
-    for i, k in enumerate(tiles):
-        loads[i].wait()
-        here = pl.ds(k, tile)
-        carry = (cent[here, :].astype(jnp.float32), jnp.ones((tile, 1), jnp.float32))
-        if n == PARTS:
-            total, found = add(0, carry, k)
-        else:
-            total, found = lax.fori_loop(0, n // PARTS, functools.partial(add, k=k), carry)
-        out[here, :] = total * (1.0 / found)
+        out[i] = total * rcp
         stores[i].start()
     for copy in stores:
         copy.wait()
@@ -249,7 +237,8 @@
     n = lax.axis_size("row")
     count, width = embeddings.shape[1:]
     k_dev = centroids.shape[1]
-    tiles = k_dev // min(128, k_dev)
+    tile = min(256, width)
+    tiles = width // tile
     vmem = pl.BlockSpec(memory_space=pltpu.VMEM)
     hbm = pl.BlockSpec(memory_space=pl.ANY)
     dma = pltpu.SemaphoreType.DMA
@@ -294,13 +283,15 @@
         in_specs=[hbm, hbm, hbm, hbm],
         out_specs=(hbm, hbm),
         scratch_shapes=[
-            pltpu.VMEM((n, count, width), jnp.bfloat16),
-            pltpu.VMEM((k_dev, width), jnp.bfloat16),
+            pltpu.VMEM((tiles, n, count, tile), jnp.bfloat16),
+            pltpu.VMEM((tiles, k_dev, tile), jnp.bfloat16),
             pltpu.VMEM((n, 1, count), jnp.int32),
-            pltpu.VMEM((k_dev, width), jnp.float32),
+            pltpu.VMEM((tiles, k_dev, tile), jnp.float32),
+            pltpu.VMEM((k_dev, n * count), jnp.bfloat16),
             dma((tiles,)),
             dma((tiles,)),
-            dma((3,)),
+            dma((tiles,)),
+            dma((2,)),
         ],
         compiler_params=pltpu.CompilerParams(vmem_limit_bytes=56 * 2**20),
     )(gathered, centroids[0], ids, gap)

time: 32.2 us -> 32.8 us (1.019)
  Pallas kernels: 31.4 us -> 32 us
    pallas_call x1, Pallas kernels: 3.47 us -> 3.99 us  [body(): pl.pallas_call(functools.partial(finish, n), out_shape=(jax.ShapeDtypeStr...]
where the time goes in v4:
time: 32.8 us; the launch traced here: 32.6 us
  Pallas kernels  32 us (98%)
  between operations  0.64 us (2%)
    pallas_call x1, Pallas kernels, body(): pl.pallas_call(functools.partial(kernel, n), out_shape=(jax.ShapeDtypeStr...  28 us
    pallas_call x1, Pallas kernels, body(): pl.pallas_call(functools.partial(finish, n), out_shape=(jax.ShapeDtypeStr...  3.99 us

profile of v4, /device:TPU:0, one launch (start us, length us, event | category | flops | bytes accessed | tf_op | source)
XLA Modules:
  0.0 32.6 jit_solution(16474237404275189157)
XLA Ops:
  0.6 28.0 %shard_map.59 = (f32[1,128]{1,0:T(1,128)}, bf16[4,128,1024]{2,1,0:T(8,128)(2,1)}, s32[4,1,128]{2,1,0:T(1,128)}) custom-call(bf16[128,1024]{1,0:T(8,128)(2,1)} %bitcast.6, bf16[512,1024]{1,0:T(8,128)(2,1)} %bitcast.4, s32[1,128]{1,0:T(1,128)} %bitcast.7, s32[1,128]{1,0:T(1,128)} %slot_hbm.1), custom_call_target="tpu_custom_call" | custom-call | tf_op jit(solution)/shard_map/pallas_call | solution.py:245
  28.6 4.0 %shard_map.60 = (f32[1,128]{1,0:T(1,128)}, f32[512,1024]{1,0:T(8,128)}) custom-call(bf16[4,128,1024]{2,1,0:T(8,128)(2,1)} %get-tuple-element.7.rows_hbm, bf16[512,1024]{1,0:T(8,128)(2,1)} %bitcast.5, s32[4,1,128]{2,1,0:T(1,128)} %get-tuple-element.8.ids_hbm, f32[1,128]{1,0:T(1,128)} %get-tuple-element.9.gap_hbm), custom_call_target="tpu_custom_call" | custom-call | tf_op jit(solution)/shard_map/pallas_call | solution.py:277

commit v5 on v3

--- a/solution.py
+++ b/solution.py
@@ -13,7 +13,7 @@
 
 def kernel(
     n, emb, cent_hbm, owner_hbm, slot_hbm, gap_out, rows_out, ids_out,
-    owner, slot, rows, cent, ids, hn, res_out, res_in,
+    owner, slot, rows, cent, ids, ids_near, hn, res_out, res_in,
     recv, send_l, send_r, id_recv, id_send, res_recv, res_send, out_sem, local,
 ):
     z = lax.axis_index("row")
@@ -128,7 +128,9 @@
     res_in[z, 0:1, :] = best
     res_in[z, 1:2, :] = chosen
     keep(z).start()
-    ids_out[...] = ids[...] - z * k_dev
+    ids_near[...] = ids[...] - z * k_dev
+    ids_copy = pltpu.make_async_copy(ids_near, ids_out, out_sem.at[n])
+    ids_copy.start()
 
     def step(s, carry):
         for c in range(PARTS):
@@ -180,13 +182,14 @@
         lambda t: remote(res_out.at[t], res_in.at[t], res_send.at[t], res_recv.at[t], t).wait()
     )
     lax.fori_loop(0, n, lambda b, carry: (keep(b).wait(), carry)[1], 0)
+    ids_copy.wait()
     got = res_in[...]
     gap_out[...] = jnp.max(got[:, 0], axis=0, keepdims=True) - jnp.sum(got[:, 1], axis=0, keepdims=True)
 
 
 def finish(
     n, rows_hbm, cent_hbm, ids_hbm, gap_hbm, gap_out, new_hbm,
-    rows, cent, ids, out, load, store, small,
+    rows, cent, ids, out, member, load_rows, load, store, small,
 ):
     k_dev = cent.shape[0]
     count = ids.shape[-1]
@@ -194,10 +197,14 @@
     tiles = range(0, k_dev, tile)
     gap_copy = pltpu.make_async_copy(gap_hbm, gap_out, small.at[0])
     ids_copy = pltpu.make_async_copy(ids_hbm, ids, small.at[1])
-    rows_copy = pltpu.make_async_copy(rows_hbm, rows, small.at[2])
-    ids_copy.start()
-    rows_copy.start()
-    gap_copy.start()
+    row_copies = [
+        pltpu.make_async_copy(
+            rows_hbm.at[pl.ds(p * n // PARTS, n // PARTS)],
+            rows.at[pl.ds(p * n // PARTS, n // PARTS)],
+            load_rows.at[p],
+        )
+        for p in range(PARTS)
+    ]
     loads = [
         pltpu.make_async_copy(cent_hbm.at[pl.ds(k, tile)], cent.at[pl.ds(k, tile)], load.at[i])
         for i, k in enumerate(tiles)
@@ -206,39 +213,46 @@
         pltpu.make_async_copy(out.at[pl.ds(k, tile)], new_hbm.at[pl.ds(k, tile)], store.at[i])
         for i, k in enumerate(tiles)
     ]
-    for copy in loads:
+    for copy in [ids_copy, *row_copies, *loads, gap_copy]:
         copy.start()
     ids_copy.wait()
-    lanes = lax.broadcasted_iota(jnp.int32, (tile, count), 0)
-
-    def members(g, k):
-        return jnp.concatenate(
-            [
-                jnp.where(lanes + k == ids[g * PARTS + j], 1.0, 0.0)
-                for j in range(PARTS)
-            ],
-            axis=1,
+    cent_ids = lax.broadcasted_iota(jnp.int32, (k_dev, count), 0)
+
+    def mark(b, found):
+        here = jnp.where(cent_ids == ids[b], 1.0, 0.0)
+        lanes = b * count if n <= 4 else pl.multiple_of(b * count, count)
+        member[:, pl.ds(lanes, count)] = here.astype(jnp.bfloat16)
+        return found + here
+
+    found = jnp.zeros((k_dev, count), jnp.float32)
+    if n <= 4:
+        for b in range(n):
+            found = mark(b, found)
+    else:
+        found = lax.fori_loop(0, n, mark, found)
+    rcp = 1.0 / (1.0 + jnp.sum(found, axis=1, keepdims=True))
+    for copy in row_copies:
+        copy.wait()
+
+    def product(k, g):
+        lanes = g * PARTS * count
+        if n > PARTS:
+            lanes = pl.multiple_of(lanes, count)
+        block = rows[pl.ds(g * PARTS, PARTS)].reshape(PARTS * count, rows.shape[-1])
+        return jnp.dot(
+            member[pl.ds(k, tile), pl.ds(lanes, PARTS * count)], block,
+            preferred_element_type=jnp.float32,
         )
 
-    def add(g, carry, k):
-        total, found = carry
-        member = members(g, k)
-        block = rows[pl.ds(g * PARTS, PARTS)].reshape(PARTS * count, rows.shape[-1])
-        total = total + jnp.dot(
-            member.astype(jnp.bfloat16), block, preferred_element_type=jnp.float32
-        )
-        return total, found + jnp.sum(member, axis=1, keepdims=True)
-
-    rows_copy.wait()
     for i, k in enumerate(tiles):
         loads[i].wait()
         here = pl.ds(k, tile)
-        carry = (cent[here, :].astype(jnp.float32), jnp.ones((tile, 1), jnp.float32))
+        total = cent[here, :].astype(jnp.float32)
         if n == PARTS:
-            total, found = add(0, carry, k)
+            total = total + product(k, 0)
         else:
-            total, found = lax.fori_loop(0, n // PARTS, functools.partial(add, k=k), carry)
-        out[here, :] = total * (1.0 / found)
+            total = lax.fori_loop(0, n // PARTS, lambda g, t: t + product(k, g), total)
+        out[here, :] = total * rcp[k:k + tile]
         stores[i].start()
     for copy in stores:
         copy.wait()
@@ -261,12 +275,13 @@
             jax.ShapeDtypeStruct((n, 1, count), jnp.int32),
         ),
         in_specs=[hbm, hbm, hbm, hbm],
-        out_specs=(vmem, hbm, vmem),
+        out_specs=(vmem, hbm, hbm),
         scratch_shapes=[
             pltpu.VMEM((1, count), jnp.int32),
             pltpu.VMEM((1, count), jnp.int32),
             pltpu.VMEM((n, count, width), jnp.bfloat16),
             pltpu.VMEM((k_dev, width), jnp.bfloat16),
+            pltpu.VMEM((n, 1, count), jnp.int32),
             pltpu.VMEM((n, 1, count), jnp.int32),
             pltpu.VMEM((k_dev, 1), jnp.float32),
             pltpu.VMEM((n, 2, count), jnp.float32),
@@ -278,7 +293,7 @@
             dma((n,)),
             dma((n,)),
             dma((n,)),
-            dma((n,)),
+            dma((n + 1,)),
             dma((3 + PARTS,)),
         ],
         compiler_params=pltpu.CompilerParams(
@@ -298,9 +313,11 @@
             pltpu.VMEM((k_dev, width), jnp.bfloat16),
             pltpu.VMEM((n, 1, count), jnp.int32),
             pltpu.VMEM((k_dev, width), jnp.float32),
+            pltpu.VMEM((k_dev, n * count), jnp.bfloat16),
+            dma((PARTS,)),
             dma((tiles,)),
             dma((tiles,)),
-            dma((3,)),
+            dma((2,)),
         ],
         compiler_params=pltpu.CompilerParams(vmem_limit_bytes=56 * 2**20),
     )(gathered, centroids[0], ids, gap)

time: 32.2 us -> 32.4 us (level)
  no operation moved by 1% of the time
where the time goes in v5:
time: 32.4 us; the launch traced here: 32.2 us
  Pallas kernels  31.6 us (98%)
  between operations  0.64 us (2%)
    pallas_call x1, Pallas kernels, body(): pl.pallas_call(functools.partial(kernel, n), out_shape=(jax.ShapeDtypeStr...  28 us
    pallas_call x1, Pallas kernels, body(): pl.pallas_call(functools.partial(finish, n), out_shape=(jax.ShapeDtypeStr...  3.63 us

profile of v5, /device:TPU:0, one launch (start us, length us, event | category | flops | bytes accessed | tf_op | source)
XLA Modules:
  0.0 32.2 jit_solution(2145960920110402626)
XLA Ops:
  0.6 28.0 %shard_map.59 = (f32[1,128]{1,0:T(1,128)}, bf16[4,128,1024]{2,1,0:T(8,128)(2,1)}, s32[4,1,128]{2,1,0:T(1,128)}) custom-call(bf16[128,1024]{1,0:T(8,128)(2,1)} %bitcast.6, bf16[512,1024]{1,0:T(8,128)(2,1)} %bitcast.4, s32[1,128]{1,0:T(1,128)} %bitcast.7, s32[1,128]{1,0:T(1,128)} %slot_hbm.1), custom_call_target="tpu_custom_call" | custom-call | tf_op jit(solution)/shard_map/pallas_call | solution.py:270
  28.6 3.6 %shard_map.60 = (f32[1,128]{1,0:T(1,128)}, f32[512,1024]{1,0:T(8,128)}) custom-call(bf16[4,128,1024]{2,1,0:T(8,128)(2,1)} %get-tuple-element.7.rows_hbm, bf16[512,1024]{1,0:T(8,128)(2,1)} %bitcast.5, s32[4,1,128]{2,1,0:T(1,128)} %get-tuple-element.8.ids_hbm, f32[1,128]{1,0:T(1,128)} %get-tuple-element.9.gap_hbm), custom_call_target="tpu_custom_call" | custom-call | tf_op jit(solution)/shard_map/pallas_call | solution.py:303

commit v6 on v3

--- a/solution.py
+++ b/solution.py
@@ -186,18 +186,21 @@
 
 def finish(
     n, rows_hbm, cent_hbm, ids_hbm, gap_hbm, gap_out, new_hbm,
-    rows, cent, ids, out, load, store, small,
+    rows, cent, ids, out, counts, load, store, small,
 ):
     k_dev = cent.shape[0]
     count = ids.shape[-1]
-    tile = min(128, k_dev)
+    tile = min(256, k_dev)
     tiles = range(0, k_dev, tile)
+    half = n // 2
     gap_copy = pltpu.make_async_copy(gap_hbm, gap_out, small.at[0])
     ids_copy = pltpu.make_async_copy(ids_hbm, ids, small.at[1])
-    rows_copy = pltpu.make_async_copy(rows_hbm, rows, small.at[2])
-    ids_copy.start()
-    rows_copy.start()
-    gap_copy.start()
+    row_copies = [
+        pltpu.make_async_copy(
+            rows_hbm.at[pl.ds(p * half, half)], rows.at[pl.ds(p * half, half)], small.at[2 + p]
+        )
+        for p in range(2)
+    ]
     loads = [
         pltpu.make_async_copy(cent_hbm.at[pl.ds(k, tile)], cent.at[pl.ds(k, tile)], load.at[i])
         for i, k in enumerate(tiles)
@@ -206,38 +209,39 @@
         pltpu.make_async_copy(out.at[pl.ds(k, tile)], new_hbm.at[pl.ds(k, tile)], store.at[i])
         for i, k in enumerate(tiles)
     ]
-    for copy in loads:
+    for copy in [ids_copy, *row_copies, *loads, gap_copy]:
         copy.start()
     ids_copy.wait()
     lanes = lax.broadcasted_iota(jnp.int32, (tile, count), 0)
 
-    def members(g, k):
-        return jnp.concatenate(
-            [
-                jnp.where(lanes + k == ids[g * PARTS + j], 1.0, 0.0)
-                for j in range(PARTS)
-            ],
-            axis=1,
+    def add(u, carry, k):
+        total, found = carry
+        member = jnp.concatenate(
+            [jnp.where(lanes + k == ids[2 * u + j], 1.0, 0.0) for j in range(2)], axis=1
         )
-
-    def add(g, carry, k):
-        total, found = carry
-        member = members(g, k)
-        block = rows[pl.ds(g * PARTS, PARTS)].reshape(PARTS * count, rows.shape[-1])
+        block = rows[pl.ds(2 * u, 2)].reshape(2 * count, rows.shape[-1])
         total = total + jnp.dot(
             member.astype(jnp.bfloat16), block, preferred_element_type=jnp.float32
         )
         return total, found + jnp.sum(member, axis=1, keepdims=True)
 
-    rows_copy.wait()
+    def add_half(p, k, carry):
+        units = half // 2
+        if units == 1:
+            return add(p, carry, k)
+        return lax.fori_loop(p * units, (p + 1) * units, functools.partial(add, k=k), carry)
+
+    row_copies[0].wait()
+    for k in tiles:
+        here = pl.ds(k, tile)
+        zero = (jnp.zeros((tile, rows.shape[-1]), jnp.float32), jnp.ones((tile, 1), jnp.float32))
+        out[here, :], counts[here, :] = add_half(0, k, zero)
+    row_copies[1].wait()
     for i, k in enumerate(tiles):
         loads[i].wait()
         here = pl.ds(k, tile)
-        carry = (cent[here, :].astype(jnp.float32), jnp.ones((tile, 1), jnp.float32))
-        if n == PARTS:
-            total, found = add(0, carry, k)
-        else:
-            total, found = lax.fori_loop(0, n // PARTS, functools.partial(add, k=k), carry)
+        carry = (out[here, :] + cent[here, :].astype(jnp.float32), counts[here, :])
+        total, found = add_half(1, k, carry)
         out[here, :] = total * (1.0 / found)
         stores[i].start()
     for copy in stores:
@@ -249,7 +253,7 @@
     n = lax.axis_size("row")
     count, width = embeddings.shape[1:]
     k_dev = centroids.shape[1]
-    tiles = k_dev // min(128, k_dev)
+    tiles = k_dev // min(256, k_dev)
     vmem = pl.BlockSpec(memory_space=pltpu.VMEM)
     hbm = pl.BlockSpec(memory_space=pl.ANY)
     dma = pltpu.SemaphoreType.DMA
@@ -298,9 +302,10 @@
             pltpu.VMEM((k_dev, width), jnp.bfloat16),
             pltpu.VMEM((n, 1, count), jnp.int32),
             pltpu.VMEM((k_dev, width), jnp.float32),
+            pltpu.VMEM((k_dev, 1), jnp.float32),
             dma((tiles,)),
             dma((tiles,)),
-            dma((3,)),
+            dma((4,)),
         ],
         compiler_params=pltpu.CompilerParams(vmem_limit_bytes=56 * 2**20),
     )(gathered, centroids[0], ids, gap)

time: 32.2 us -> 32 us (level)
  no operation moved by 1% of the time
where the time goes in v6:
time: 32 us; the launch traced here: 31.8 us
  Pallas kernels  31.2 us (98%)
  between operations  0.64 us (2%)
    pallas_call x1, Pallas kernels, body(): pl.pallas_call(functools.partial(kernel, n), out_shape=(jax.ShapeDtypeStr...  28 us
    pallas_call x1, Pallas kernels, body(): pl.pallas_call(functools.partial(finish, n), out_shape=(jax.ShapeDtypeStr...  3.23 us

profile of v6, /device:TPU:0, one launch (start us, length us, event | category | flops | bytes accessed | tf_op | source)
XLA Modules:
  0.0 31.8 jit_solution(726157098095712526)
XLA Ops:
  0.6 28.0 %shard_map.59 = (f32[1,128]{1,0:T(1,128)}, bf16[4,128,1024]{2,1,0:T(8,128)(2,1)}, s32[4,1,128]{2,1,0:T(1,128)}) custom-call(bf16[128,1024]{1,0:T(8,128)(2,1)} %bitcast.6, bf16[512,1024]{1,0:T(8,128)(2,1)} %bitcast.4, s32[1,128]{1,0:T(1,128)} %bitcast.7, s32[1,128]{1,0:T(1,128)} %slot_hbm.1), custom_call_target="tpu_custom_call" | custom-call | tf_op jit(solution)/shard_map/pallas_call | solution.py:260
  28.6 3.2 %shard_map.60 = (f32[1,128]{1,0:T(1,128)}, f32[512,1024]{1,0:T(8,128)}) custom-call(bf16[4,128,1024]{2,1,0:T(8,128)(2,1)} %get-tuple-element.7.rows_hbm, bf16[512,1024]{1,0:T(8,128)(2,1)} %bitcast.5, s32[4,1,128]{2,1,0:T(1,128)} %get-tuple-element.8.ids_hbm, f32[1,128]{1,0:T(1,128)} %get-tuple-element.9.gap_hbm), custom_call_target="tpu_custom_call" | custom-call | tf_op jit(solution)/shard_map/pallas_call | solution.py:292
